TPU v7x, 32 devices: a whole 2x2x4 slice. The times are simulated.
32 devices in a mesh: jobs: 2 (over x), seq: 16 (over z, y, core).
Axes of the slice: x: 2, y: 2, z: 4, core: 2. Of those that a mesh axis runs over, the one named last changes fastest.
Arguments:
- queries: bfloat16 [1024, 4096], P(('jobs', 'seq')), parts along dimension 0, may hold values from -12 to 12
- keys: bfloat16 [1024, 4096], P(('jobs', 'seq')), parts along dimension 0, may hold values from -6 to 6
- values: bfloat16 [1024, 4096], P(('jobs', 'seq')), parts along dimension 0, may hold values from -6 to 6
- live_counts: int32 [2, 16], P('jobs', 'seq'), parts along dimension 0, may hold values from 4 to 16, as said below
- merge_dest: int32 [2, 1024], P('jobs', 'seq'), parts along dimension 0, may hold values from 0 to 15, as said below
- latents: float32 [2, 1024, 64], P('jobs', 'seq'), parts along dimension 0, may hold values from -6 to 6
- guidance: float32 [2], P('jobs'), parts along dimension 0, may hold values from 3 to 6
- step_index: int32 [2], P('jobs'), parts along dimension 0, may hold values from 0 to 980
- out_weight: bfloat16 [4096, 64], replicated, may hold values from -0.09375 to 0.09375
Outputs:
- denoised: float32 [2, 1024, 64], P('jobs', 'seq'), parts along dimension 0
- merged_next: float32 [2, 256, 64], P('jobs', 'seq'), parts along dimension 0
There are 2 independent parts, one for each index of `jobs`. A program takes and returns all parts, laid end to end along the dimension named above; an argument that names none is the same for every part. Nothing has to cross between parts.
Inputs may be any that keep to these rules, and one draw needn't show every extreme that they name: `live_counts`: in every video some merge group has exactly 16 live slots. `merge_dest`: each token names a slot of its own merge group below that group's live count, and every live slot is named by at least one token.
All inputs are finite; a program needn't handle non-finite values.
Results may differ from a plain program's by a relative error of at most 0.0031.
Values may be sent and summed in bfloat16 or wider, within the bound.
A program may use at most 64 MiB of HBM per device.

v0:
```python
import functools
import math

import jax
import jax.numpy as jnp
from jax import lax
from jax.experimental import pallas as pl
from jax.experimental.pallas import tpu as pltpu
from jax.sharding import PartitionSpec as P

HEADS = 32
HD = 128
TIMESTEPS = 1000
STRIDE = 20
NEG_BIG = -1e30
SHIFT = 5.0
MESH = pl.DeviceIdType.MESH


def sigma_of(step_value):
    frac = 1.0 - step_value / TIMESTEPS
    return SHIFT * frac / (1.0 + (SHIFT - 1.0) * frac)


def sweep(first, last, body):
    if last - first <= 16:
        for index in range(first, last):
            body(index)
    else:

        def step(index, carry):
            body(index)
            return carry

        lax.fori_loop(first, last, step, 0)


def kernel(
    n,
    items,
    videos,
    query_hbm,
    key_hbm,
    value_hbm,
    dest_ref,
    latent_hbm,
    weight_hbm,
    velocity_ref,
    slot_ref,
    heads_buf,
    own,
    count_pair,
    count_buf,
    weight_twice,
    weight_rows,
    latent_buf,
    total,
    stage,
    parts,
    part_recv,
    small_sems,
    head_recv,
    send_sems,
    own_sems,
    pair_recv,
    vouched,
):
    half = n // 2
    me = lax.axis_index("seq")
    branch = me // half
    rank = me % half
    base = branch * half
    rows = query_hbm.shape[0]
    cap = rows // 2
    keys_total = half * rows
    channels = weight_hbm.shape[0]
    scale = 1.0 / math.sqrt(HD)
    sources = (query_hbm, key_hbm, value_hbm)

    barrier = pltpu.get_barrier_semaphore()

    partner = (me + half) % n

    def greet(p):
        pl.semaphore_signal(
            barrier,
            inc=1,
            device_id={"seq": base + (rank + p) % half},
            device_id_type=MESH,
        )

    sweep(1, half, greet)
    pl.semaphore_signal(barrier, inc=1, device_id={"seq": partner}, device_id_type=MESH)

    head_col = pl.multiple_of(((rank * items) % HEADS) * HD, HD)
    weight_own = weight_hbm.at[:, pl.ds(head_col, items * HD)]
    small_copies = [
        pltpu.make_async_copy(weight_own, weight_twice.at[pl.ds(0, channels)], small_sems.at[0]),
        pltpu.make_async_copy(
            weight_own, weight_twice.at[pl.ds(channels, channels)], small_sems.at[1]
        ),
        pltpu.make_async_copy(latent_hbm, latent_buf, small_sems.at[2]),
    ]
    row_at = pl.multiple_of(rank * rows, rows)

    def heads_of(which, peer, item):
        column = pl.multiple_of((peer * items + item) * HD, HD)
        return own.at[which, :, pl.ds(column, HD)]

    own_copies = [
        pltpu.make_async_copy(sources[which], own.at[which], own_sems.at[which])
        for which in range(3)
    ]
    for copy in own_copies:
        copy.start()

    count = jnp.max(dest_ref[...].astype(jnp.float32), axis=1, keepdims=True) + 1.0
    count_pair[0] = jnp.broadcast_to(count, (videos, 128)).astype(jnp.int32)
    for copy in own_copies:
        copy.wait()

    pl.semaphore_wait(barrier, half)

    partner_copy = pltpu.make_async_remote_copy(
        src_ref=count_pair.at[0],
        dst_ref=count_pair.at[1],
        send_sem=send_sems.at[0],
        recv_sem=pair_recv,
        device_id={"seq": partner},
        device_id_type=MESH,
    )
    partner_copy.start()

    def send_count(p):
        pltpu.make_async_remote_copy(
            src_ref=count_pair,
            dst_ref=count_buf.at[rank],
            send_sem=send_sems.at[3],
            recv_sem=part_recv.at[0],
            device_id={"seq": base + (rank + p) % half},
            device_id_type=MESH,
        ).start()

    for item in range(items):

        def send_heads(p):
            peer = (rank + p) % half
            for which in range(3):
                pltpu.make_async_remote_copy(
                    src_ref=heads_of(which, peer, item),
                    dst_ref=heads_buf.at[item, which, pl.ds(row_at, rows)],
                    send_sem=send_sems.at[1],
                    recv_sem=head_recv.at[item],
                    device_id={"seq": base + peer},
                    device_id_type=MESH,
                ).start()

        sweep(1, half, send_heads)

        if item == 0:
            partner_copy.wait()
            pltpu.make_async_copy(count_pair, count_buf.at[rank], part_recv.at[0]).start()
            sweep(1, half, send_count)

    for item in range(items):
        for which in range(3):
            pltpu.make_async_copy(
                heads_of(which, rank, item),
                heads_buf.at[item, which, pl.ds(row_at, rows)],
                head_recv.at[item],
            ).start()
    for copy in small_copies:
        copy.start()

    def vouch(p):
        pl.semaphore_signal(
            vouched,
            inc=1,
            device_id={"seq": base + (rank + p) % half},
            device_id_type=MESH,
        )

    sweep(1, half, vouch)

    for copy in small_copies:
        copy.wait()
    weight_rows[...] = weight_twice[...].astype(jnp.float32).T.astype(jnp.bfloat16)

    tokens = latent_buf.shape[1]
    slot_hots, latent_means, shares = [], [], []
    for v in range(videos):
        hot = lax.broadcasted_iota(jnp.int32, (cap, tokens), 0) == dest_ref[v : v + 1, :]
        hot = hot.astype(jnp.float32)
        latent_sum = jnp.dot(
            hot,
            latent_buf[v],
            precision=lax.Precision.HIGHEST,
            preferred_element_type=jnp.float32,
        )
        tally = jnp.sum(hot, axis=1, keepdims=True)
        inverse = 1.0 / jnp.maximum(tally, 1.0)
        slot_hots.append(hot)
        latent_means.append(latent_sum * inverse)
        shares.append(tally * inverse)

    pltpu.make_async_copy(count_buf, count_buf, part_recv.at[0]).wait()
    video = (rank * items) // HEADS
    lane = lax.broadcasted_iota(jnp.int32, (1, keys_total), 1)
    group_of = ((lane % rows) // cap) * half + lane // rows
    place_of = lane % cap

    def count_step(r, held):
        pair = count_buf[r]
        for side in range(2):
            row = pair[side, 0:1]
            for v in range(1, videos):
                row = jnp.where(video == v, pair[side, v : v + 1], row)
            wide = jnp.concatenate([row] * (keys_total // 128), axis=1)
            owner = (side * half + base) % n + r
            held = jnp.where(group_of == owner, wide, held)
        return held

    held = jnp.zeros((1, keys_total), jnp.int32)
    if half <= 16:
        for r in range(half):
            held = count_step(r, held)
    else:
        held = lax.fori_loop(0, half, count_step, held)
    live = place_of < held

    def by_blocks(block, body):
        if keys_total <= 4 * block:
            for index in range(keys_total // block):
                body(index)
        else:

            def step(index, carry):
                body(index)
                return carry

            lax.fori_loop(0, keys_total // block, step, 0)

    left = lax.broadcasted_iota(jnp.int32, (cap // 2, 2 * channels), 1) < channels

    for item in range(items):
        pltpu.make_async_copy(heads_buf.at[item], heads_buf.at[item], head_recv.at[item]).wait()

        block = min(keys_total, 256)

        def attend(index):
            at = pl.ds(pl.multiple_of(index * block, block), block)
            scores = (
                lax.dot_general(
                    heads_buf[item, 0, at, :],
                    heads_buf[item, 1],
                    (((1,), (1,)), ((), ())),
                    preferred_element_type=jnp.float32,
                )
                * scale
            )
            scores = jnp.where(live, scores, NEG_BIG)
            weights = jnp.exp(scores - jnp.max(scores, axis=-1, keepdims=True))
            inverse = 1.0 / jnp.sum(weights, axis=-1, keepdims=True)
            probs = (weights * inverse).astype(jnp.bfloat16)
            attended = jnp.dot(
                probs, heads_buf[item, 2], preferred_element_type=jnp.float32
            ).astype(jnp.bfloat16)
            term = jnp.dot(
                attended,
                weight_rows[item * HD : (item + 1) * HD, :],
                preferred_element_type=jnp.float32,
            )
            if item == 0:
                total[at, :] = term
            else:
                total[at, :] += term

        by_blocks(block, attend)

    both = total[...].reshape(half, 2, 2, cap // 2, 2 * channels)
    stage[...] = jnp.where(left, both[:, :, 0], both[:, :, 1])

    pl.semaphore_wait(vouched, half - 1)

    def send_part(p):
        owner = (me + p) % n
        pltpu.make_async_remote_copy(
            src_ref=stage.at[owner % half, owner // half],
            dst_ref=parts.at[me],
            send_sem=send_sems.at[2],
            recv_sem=part_recv.at[1],
            device_id={"seq": owner},
            device_id_type=MESH,
        ).start()

    sweep(1, n, send_part)
    pltpu.make_async_copy(stage.at[rank, branch], parts.at[me], part_recv.at[1]).start()
    pltpu.make_async_copy(parts, parts, part_recv.at[1]).wait()

    span = half // videos
    for v in range(videos):
        cond = jnp.sum(parts[v * span : (v + 1) * span], axis=0)
        uncond = jnp.sum(parts[half + v * span : half + (v + 1) * span], axis=0)
        merged = jnp.concatenate(
            [
                jnp.where(left, cond, pltpu.roll(uncond, channels, 1)),
                jnp.where(left, pltpu.roll(cond, channels, 1), uncond),
            ],
            axis=0,
        )
        velocity = lax.dot_general(
            slot_hots[v],
            merged,
            (((0,), (0,)), ((), ())),
            precision=lax.Precision.HIGHEST,
            preferred_element_type=jnp.float32,
        )
        velocity_ref[0, v] = velocity[:, :channels]
        velocity_ref[1, v] = velocity[:, channels:]
        merged = shares[v] * merged
        slot_ref[0, v] = merged[:, :channels]
        slot_ref[1, v] = merged[:, channels:]
        slot_ref[2, v] = latent_means[v]

    pltpu.make_async_copy(
        count_buf.at[pl.ds(0, half - 1)], count_buf.at[pl.ds(0, half - 1)], send_sems.at[3]
    ).wait()
    sent = heads_buf.at[:, :, pl.ds(0, (half - 1) * rows)]
    pltpu.make_async_copy(sent, sent, send_sems.at[1]).wait()
    pltpu.make_async_copy(
        parts.at[pl.ds(0, n - 1)], parts.at[pl.ds(0, n - 1)], send_sems.at[2]
    ).wait()


def local(
    queries, keys, values, live_counts, merge_dest, latents, guidance, step_index, out_weight
):
    n = lax.axis_size("seq")
    half = n // 2
    rows, columns = queries.shape
    videos, tokens, channels = latents.shape
    items = columns // HD // half
    cap = rows // 2
    outside = pl.BlockSpec(memory_space=pltpu.HBM)
    inside = pl.BlockSpec(memory_space=pltpu.VMEM)
    velocities, slots = pl.pallas_call(
        functools.partial(kernel, n, items, videos),
        out_shape=(
            jax.ShapeDtypeStruct((2, videos, tokens, channels), jnp.float32),
            jax.ShapeDtypeStruct((3, videos, cap, channels), jnp.float32),
        ),
        in_specs=[outside] * 3 + [inside] + [outside] * 2,
        out_specs=(inside, inside),
        scratch_shapes=[
            pltpu.VMEM((items, 3, half * rows, HD), jnp.bfloat16),
            pltpu.VMEM((3, rows, columns), jnp.bfloat16),
            pltpu.VMEM((2, videos, 128), jnp.int32),
            pltpu.VMEM((half, 2, videos, 128), jnp.int32),
            pltpu.VMEM((2 * channels, items * HD), jnp.bfloat16),
            pltpu.VMEM((items * HD, 2 * channels), jnp.bfloat16),
            pltpu.VMEM((videos, tokens, channels), jnp.float32),
            pltpu.VMEM((half * rows, 2 * channels), jnp.float32),
            pltpu.VMEM((half, 2, cap // 2, 2 * channels), jnp.float32),
            pltpu.VMEM((n, cap // 2, 2 * channels), jnp.float32),
            pltpu.SemaphoreType.DMA((2,)),
            pltpu.SemaphoreType.DMA((3,)),
            pltpu.SemaphoreType.DMA((items,)),
            pltpu.SemaphoreType.DMA((4,)),
            pltpu.SemaphoreType.DMA((3,)),
            pltpu.SemaphoreType.DMA,
            pltpu.SemaphoreType.REGULAR,
        ],
        compiler_params=pltpu.CompilerParams(
            collective_id=0, has_side_effects=True, vmem_limit_bytes=55040 * 1024
        ),
    )(
        queries,
        keys,
        values,
        merge_dest,
        latents,
        out_weight.T,
    )
    step_value = step_index.astype(jnp.float32)
    sigma_now = sigma_of(step_value)
    sigma_next = sigma_of(step_value + float(STRIDE))
    gain = guidance[:, None, None]
    velocity = velocities[1] + gain * (velocities[0] - velocities[1])
    denoised = latents - sigma_now[:, None, None] * velocity
    merged = slots[1] + gain * (slots[0] - slots[1])
    merged_next = slots[2] + (sigma_next - sigma_now)[:, None, None] * merged
    return denoised, merged_next


def solution(mesh):
    placed = (
        P(("jobs", "seq"), None),
        P(("jobs", "seq"), None),
        P(("jobs", "seq"), None),
        P("jobs", "seq"),
        P("jobs", "seq"),
        P("jobs", "seq", None),
        P("jobs"),
        P("jobs"),
        P(),
    )
    return jax.shard_map(
        local,
        mesh=mesh,
        in_specs=placed,
        out_specs=(P("jobs", "seq", None), P("jobs", "seq", None)),
        check_vma=False,
    )
```

profile of v0, /device:TPU:0, one launch (start us, length us, event | category | flops | bytes accessed | tf_op | source)
XLA Modules:
  0.0 24.8 jit_solution(760115821034271073)
XLA Ops:
  0.6 0.0 copy-start
  1.4 0.0 copy-start.1
  1.4 0.0 copy-done
  1.4 0.6 %copy-done.1 = s32[1,64]{1,0:T(1,128)S(1)} copy-done((s32[1,64]{1,0:T(1,128)S(1)}, s32[1,64]{1,0:T(1,128)}, u32[]{:S(2)}) %copy-start.1) | copy-done | bytes 280
  2.0 20.9 %shard_map.95 = (f32[2,1,64,64]{3,2,1,0:T(8,128)S(1)}, f32[3,1,16,64]{3,2,1,0:T(8,128)S(1)}) custom-call(bf16[32,4096]{1,0:T(8,128)(2,1)} %query_hbm.1, bf16[32,4096]{1,0:T(8,128)(2,1)} %key_hbm.1, bf16[32,4096]{1,0:T(8,128)(2,1)} %value_hbm.1, s32[1,64]{1,0:T(1,128)S(1)} %copy-done.1, f32[1,64,64]{2,1,0:T(8,128)S(1)} %copy-done, bf16[64,4096]{1,0:T(8,128)(2,1)} %bitcast.32), custom_call_target="tpu_custom_call" | custom-call | tf_op jit(solution)/shard_map/pallas_call | solution.py:346
  23.6 0.6 %fusion.7 = f32[1,16,64]{2,1,0:T(8,128)} fusion(f32[3,1,16,64]{3,2,1,0:T(8,128)S(1)} %get-tuple-element.5, f32[]{:T(128)} %bitcast.31, f32[]{:T(128)} %bitcast.6), kind=kLoop, calls=%fused_computation.9 | loop fusion | flops 5120 | bytes 16392 | tf_op jit(solution)/shard_map/add | solution.py:391
  24.2 0.6 %fusion.3 = f32[1,64,64]{2,1,0:T(8,128)} fusion(f32[1,64,64]{2,1,0:T(8,128)S(1)} %copy-done, f32[2,1,64,64]{3,2,1,0:T(8,128)S(1)} %get-tuple-element.4, f32[]{:T(128)} %bitcast.30, f32[]{:T(128)} %bitcast), kind=kLoop, calls=%fused_computation.4 | loop fusion | flops 20480 | bytes 65544 | tf_op jit(solution)/shard_map/sub | solution.py:389
Async XLA Ops:
  0.6 0.8 %copy-start = (f32[1,64,64]{2,1,0:T(8,128)S(1)}, f32[1,64,64]{2,1,0:T(8,128)}, u32[]{:S(2)}) copy-start(f32[1,64,64]{2,1,0:T(8,128)} %latent_hbm.1) | copy-start | bytes 49156
  1.4 0.7 %copy-start.1 = (s32[1,64]{1,0:T(1,128)S(1)}, s32[1,64]{1,0:T(1,128)}, u32[]{:S(2)}) copy-start(s32[1,64]{1,0:T(1,128)} %dest_ref.1) | copy-start | bytes 772
where the time goes:
time: 25.1 us; the launch traced here: 24.8 us
  Pallas kernels  20.9 us (83%)
  between operations  2.05 us (8%)
  other arithmetic  1.23 us (5%)
  local copies, waits for them, and re-layouts  0.65 us (3%)
    pallas_call x1, Pallas kernels, local(): pl.pallas_call(functools.partial(kernel, n, items, videos), out_shape=(ja...  20.9 us
    unnamed x4, local copies, waits for them, and re-layouts  0.65 us
    sub x1, other arithmetic, local(): denoised = latents - sigma_now[:, None, None] * velocity  0.62 us
    add x1, other arithmetic, local(): merged_next = slots[2] + (sigma_next - sigma_now)[:, None, None] * merged  0.61 us

commit v1 on v0

--- a/solution.py
+++ b/solution.py
@@ -22,8 +22,8 @@
     return SHIFT * frac / (1.0 + (SHIFT - 1.0) * frac)
 
 
-def sweep(first, last, body):
-    if last - first <= 16:
+def sweep(first, last, body, longest=16):
+    if last - first <= longest:
         for index in range(first, last):
             body(index)
     else:
@@ -49,6 +49,7 @@
     slot_ref,
     heads_buf,
     own,
+    laid,
     count_pair,
     count_buf,
     weight_twice,
@@ -70,7 +71,7 @@
     branch = me // half
     rank = me % half
     base = branch * half
-    rows = query_hbm.shape[0]
+    rows, columns = query_hbm.shape
     cap = rows // 2
     keys_total = half * rows
     channels = weight_hbm.shape[0]
@@ -101,11 +102,6 @@
         ),
         pltpu.make_async_copy(latent_hbm, latent_buf, small_sems.at[2]),
     ]
-    row_at = pl.multiple_of(rank * rows, rows)
-
-    def heads_of(which, peer, item):
-        column = pl.multiple_of((peer * items + item) * HD, HD)
-        return own.at[which, :, pl.ds(column, HD)]
 
     own_copies = [
         pltpu.make_async_copy(sources[which], own.at[which], own_sems.at[which])
@@ -118,6 +114,13 @@
     count_pair[0] = jnp.broadcast_to(count, (videos, 128)).astype(jnp.int32)
     for copy in own_copies:
         copy.wait()
+
+    def lay(head):
+        for which in range(3):
+            column = head * HD if isinstance(head, int) else pl.multiple_of(head * HD, HD)
+            laid[head, which] = own[which, :, pl.ds(column, HD)]
+
+    sweep(0, columns // HD, lay, 32)
 
     pl.semaphore_wait(barrier, half)
 
@@ -145,15 +148,14 @@
 
         def send_heads(p):
             peer = (rank + p) % half
-            for which in range(3):
-                pltpu.make_async_remote_copy(
-                    src_ref=heads_of(which, peer, item),
-                    dst_ref=heads_buf.at[item, which, pl.ds(row_at, rows)],
-                    send_sem=send_sems.at[1],
-                    recv_sem=head_recv.at[item],
-                    device_id={"seq": base + peer},
-                    device_id_type=MESH,
-                ).start()
+            pltpu.make_async_remote_copy(
+                src_ref=laid.at[peer * items + item],
+                dst_ref=heads_buf.at[item, rank],
+                send_sem=send_sems.at[1],
+                recv_sem=head_recv.at[item],
+                device_id={"seq": base + peer},
+                device_id_type=MESH,
+            ).start()
 
         sweep(1, half, send_heads)
 
@@ -163,12 +165,9 @@
             sweep(1, half, send_count)
 
     for item in range(items):
-        for which in range(3):
-            pltpu.make_async_copy(
-                heads_of(which, rank, item),
-                heads_buf.at[item, which, pl.ds(row_at, rows)],
-                head_recv.at[item],
-            ).start()
+        pltpu.make_async_copy(
+            laid.at[rank * items + item], heads_buf.at[item, rank], head_recv.at[item]
+        ).start()
     for copy in small_copies:
         copy.start()
 
@@ -199,7 +198,7 @@
         )
         tally = jnp.sum(hot, axis=1, keepdims=True)
         inverse = 1.0 / jnp.maximum(tally, 1.0)
-        slot_hots.append(hot)
+        slot_hots.append(jnp.concatenate([hot.T] * 3, axis=1).astype(jnp.bfloat16))
         latent_means.append(latent_sum * inverse)
         shares.append(tally * inverse)
 
@@ -247,12 +246,17 @@
 
         block = min(keys_total, 256)
 
+        key_rows = heads_buf[item, :, 1].reshape(keys_total, HD)
+        value_rows = heads_buf[item, :, 2].reshape(keys_total, HD)
+        ranks = block // rows
+
         def attend(index):
             at = pl.ds(pl.multiple_of(index * block, block), block)
+            query_rows = heads_buf[item, pl.ds(index * ranks, ranks), 0].reshape(block, HD)
             scores = (
                 lax.dot_general(
-                    heads_buf[item, 0, at, :],
-                    heads_buf[item, 1],
+                    query_rows,
+                    key_rows,
                     (((1,), (1,)), ((), ())),
                     preferred_element_type=jnp.float32,
                 )
@@ -263,7 +267,7 @@
             inverse = 1.0 / jnp.sum(weights, axis=-1, keepdims=True)
             probs = (weights * inverse).astype(jnp.bfloat16)
             attended = jnp.dot(
-                probs, heads_buf[item, 2], preferred_element_type=jnp.float32
+                probs, value_rows, preferred_element_type=jnp.float32
             ).astype(jnp.bfloat16)
             term = jnp.dot(
                 attended,
@@ -282,18 +286,18 @@
 
     pl.semaphore_wait(vouched, half - 1)
 
-    def send_part(p):
-        owner = (me + p) % n
+    def send_part(side, peer):
         pltpu.make_async_remote_copy(
-            src_ref=stage.at[owner % half, owner // half],
+            src_ref=stage.at[peer, side],
             dst_ref=parts.at[me],
             send_sem=send_sems.at[2],
             recv_sem=part_recv.at[1],
-            device_id={"seq": owner},
+            device_id={"seq": side * half + peer},
             device_id_type=MESH,
         ).start()
 
-    sweep(1, n, send_part)
+    sweep(0, half, lambda p: send_part(1 - branch, (rank + p) % half))
+    sweep(1, half, lambda p: send_part(branch, (rank + p) % half))
     pltpu.make_async_copy(stage.at[rank, branch], parts.at[me], part_recv.at[1]).start()
     pltpu.make_async_copy(parts, parts, part_recv.at[1]).wait()
 
@@ -308,11 +312,13 @@
             ],
             axis=0,
         )
-        velocity = lax.dot_general(
+        terms, rest = [], merged
+        for _ in range(3):
+            terms.append(rest.astype(jnp.bfloat16))
+            rest = rest - terms[-1].astype(jnp.float32)
+        velocity = jnp.dot(
             slot_hots[v],
-            merged,
-            (((0,), (0,)), ((), ())),
-            precision=lax.Precision.HIGHEST,
+            jnp.concatenate(terms, axis=0),
             preferred_element_type=jnp.float32,
         )
         velocity_ref[0, v] = velocity[:, :channels]
@@ -325,7 +331,7 @@
     pltpu.make_async_copy(
         count_buf.at[pl.ds(0, half - 1)], count_buf.at[pl.ds(0, half - 1)], send_sems.at[3]
     ).wait()
-    sent = heads_buf.at[:, :, pl.ds(0, (half - 1) * rows)]
+    sent = heads_buf.at[:, pl.ds(0, half - 1)]
     pltpu.make_async_copy(sent, sent, send_sems.at[1]).wait()
     pltpu.make_async_copy(
         parts.at[pl.ds(0, n - 1)], parts.at[pl.ds(0, n - 1)], send_sems.at[2]
@@ -352,8 +358,9 @@
         in_specs=[outside] * 3 + [inside] + [outside] * 2,
         out_specs=(inside, inside),
         scratch_shapes=[
-            pltpu.VMEM((items, 3, half * rows, HD), jnp.bfloat16),
+            pltpu.VMEM((items, half, 3, rows, HD), jnp.bfloat16),
             pltpu.VMEM((3, rows, columns), jnp.bfloat16),
+            pltpu.VMEM((columns // HD, 3, rows, HD), jnp.bfloat16),
             pltpu.VMEM((2, videos, 128), jnp.int32),
             pltpu.VMEM((half, 2, videos, 128), jnp.int32),
             pltpu.VMEM((2 * channels, items * HD), jnp.bfloat16),

time: 25.1 us -> 25.2 us (level)
  no operation moved by 1% of the time
where the time goes in v1:
time: 25.2 us; the launch traced here: 24.9 us
  Pallas kernels  21 us (83%)
  between operations  2.05 us (8%)
  other arithmetic  1.23 us (5%)
  local copies, waits for them, and re-layouts  0.65 us (3%)
    pallas_call x1, Pallas kernels, local(): pl.pallas_call(functools.partial(kernel, n, items, videos), out_shape=(ja...  21 us
    unnamed x4, local copies, waits for them, and re-layouts  0.65 us
    sub x1, other arithmetic, local(): denoised = latents - sigma_now[:, None, None] * velocity  0.62 us
    add x1, other arithmetic, local(): merged_next = slots[2] + (sigma_next - sigma_now)[:, None, None] * merged  0.61 us

profile of v1, /device:TPU:0, one launch (start us, length us, event | category | flops | bytes accessed | tf_op | source)
XLA Modules:
  0.0 24.9 jit_solution(8020667386828220197)
XLA Ops:
  0.6 0.0 copy-start
  1.4 0.0 copy-start.1
  1.4 0.0 copy-done
  1.4 0.6 %copy-done.1 = s32[1,64]{1,0:T(1,128)S(1)} copy-done((s32[1,64]{1,0:T(1,128)S(1)}, s32[1,64]{1,0:T(1,128)}, u32[]{:S(2)}) %copy-start.1) | copy-done | bytes 280
  2.0 21.0 %shard_map.95 = (f32[2,1,64,64]{3,2,1,0:T(8,128)S(1)}, f32[3,1,16,64]{3,2,1,0:T(8,128)S(1)}) custom-call(bf16[32,4096]{1,0:T(8,128)(2,1)} %query_hbm.1, bf16[32,4096]{1,0:T(8,128)(2,1)} %key_hbm.1, bf16[32,4096]{1,0:T(8,128)(2,1)} %value_hbm.1, s32[1,64]{1,0:T(1,128)S(1)} %copy-done.1, f32[1,64,64]{2,1,0:T(8,128)S(1)} %copy-done, bf16[64,4096]{1,0:T(8,128)(2,1)} %bitcast.32), custom_call_target="tpu_custom_call" | custom-call | tf_op jit(solution)/shard_map/pallas_call | solution.py:352
  23.7 0.6 %fusion.7 = f32[1,16,64]{2,1,0:T(8,128)} fusion(f32[3,1,16,64]{3,2,1,0:T(8,128)S(1)} %get-tuple-element.5, f32[]{:T(128)} %bitcast.31, f32[]{:T(128)} %bitcast.6), kind=kLoop, calls=%fused_computation.9 | loop fusion | flops 5120 | bytes 16392 | tf_op jit(solution)/shard_map/add | solution.py:398
  24.3 0.6 %fusion.3 = f32[1,64,64]{2,1,0:T(8,128)} fusion(f32[1,64,64]{2,1,0:T(8,128)S(1)} %copy-done, f32[2,1,64,64]{3,2,1,0:T(8,128)S(1)} %get-tuple-element.4, f32[]{:T(128)} %bitcast.30, f32[]{:T(128)} %bitcast), kind=kLoop, calls=%fused_computation.4 | loop fusion | flops 20480 | bytes 65544 | tf_op jit(solution)/shard_map/sub | solution.py:396
Async XLA Ops:
  0.6 0.8 %copy-start = (f32[1,64,64]{2,1,0:T(8,128)S(1)}, f32[1,64,64]{2,1,0:T(8,128)}, u32[]{:S(2)}) copy-start(f32[1,64,64]{2,1,0:T(8,128)} %latent_hbm.1) | copy-start | bytes 49156
  1.4 0.7 %copy-start.1 = (s32[1,64]{1,0:T(1,128)S(1)}, s32[1,64]{1,0:T(1,128)}, u32[]{:S(2)}) copy-start(s32[1,64]{1,0:T(1,128)} %dest_ref.1) | copy-start | bytes 772

commit v2 on v1

--- a/solution.py
+++ b/solution.py
@@ -144,10 +144,21 @@
             device_id_type=MESH,
         ).start()
 
+    bits = (half - 1).bit_length()
+    core = rank % 2
+
+    def peer_at(p):
+        if half != 1 << bits or half < 4:
+            return (rank + p) % half
+        away, other = p // 2, p % 2
+        turned = sum(((away // 2**k) % 2) * 2 ** (bits - 2 - k) for k in range(bits - 1))
+        step = 2 * (away * (1 - core) + turned * core) + other
+        return sum(((rank // 2**k + step // 2**k) % 2) * 2**k for k in range(bits))
+
     for item in range(items):
 
         def send_heads(p):
-            peer = (rank + p) % half
+            peer = peer_at(p)
             pltpu.make_async_remote_copy(
                 src_ref=laid.at[peer * items + item],
                 dst_ref=heads_buf.at[item, rank],
@@ -157,7 +168,8 @@
                 device_id_type=MESH,
             ).start()
 
-        sweep(1, half, send_heads)
+        sweep(2, half, send_heads)
+        send_heads(1)
 
         if item == 0:
             partner_copy.wait()

time: 25.2 us -> 25.2 us (level)
  no operation moved by 1% of the time
where the time goes in v2:
time: 25.2 us; the launch traced here: 24.9 us
  Pallas kernels  20.9 us (83%)
  between operations  2.05 us (8%)
  other arithmetic  1.23 us (5%)
  local copies, waits for them, and re-layouts  0.65 us (3%)
    pallas_call x1, Pallas kernels, local(): pl.pallas_call(functools.partial(kernel, n, items, videos), out_shape=(ja...  20.9 us
    unnamed x4, local copies, waits for them, and re-layouts  0.65 us
    sub x1, other arithmetic, local(): denoised = latents - sigma_now[:, None, None] * velocity  0.62 us
    add x1, other arithmetic, local(): merged_next = slots[2] + (sigma_next - sigma_now)[:, None, None] * merged  0.61 us

profile of v2, /device:TPU:0, one launch (start us, length us, event | category | flops | bytes accessed | tf_op | source)
XLA Modules:
  0.0 24.9 jit_solution(6327327393824812390)
XLA Ops:
  0.6 0.0 copy-start
  1.4 0.0 copy-start.1
  1.4 0.0 copy-done
  1.4 0.6 %copy-done.1 = s32[1,64]{1,0:T(1,128)S(1)} copy-done((s32[1,64]{1,0:T(1,128)S(1)}, s32[1,64]{1,0:T(1,128)}, u32[]{:S(2)}) %copy-start.1) | copy-done | bytes 280
  2.0 20.9 %shard_map.95 = (f32[2,1,64,64]{3,2,1,0:T(8,128)S(1)}, f32[3,1,16,64]{3,2,1,0:T(8,128)S(1)}) custom-call(bf16[32,4096]{1,0:T(8,128)(2,1)} %query_hbm.1, bf16[32,4096]{1,0:T(8,128)(2,1)} %key_hbm.1, bf16[32,4096]{1,0:T(8,128)(2,1)} %value_hbm.1, s32[1,64]{1,0:T(1,128)S(1)} %copy-done.1, f32[1,64,64]{2,1,0:T(8,128)S(1)} %copy-done, bf16[64,4096]{1,0:T(8,128)(2,1)} %bitcast.32), custom_call_target="tpu_custom_call" | custom-call | tf_op jit(solution)/shard_map/pallas_call | solution.py:364
  23.7 0.6 %fusion.7 = f32[1,16,64]{2,1,0:T(8,128)} fusion(f32[3,1,16,64]{3,2,1,0:T(8,128)S(1)} %get-tuple-element.5, f32[]{:T(128)} %bitcast.31, f32[]{:T(128)} %bitcast.6), kind=kLoop, calls=%fused_computation.9 | loop fusion | flops 5120 | bytes 16392 | tf_op jit(solution)/shard_map/add | solution.py:410
  24.3 0.6 %fusion.3 = f32[1,64,64]{2,1,0:T(8,128)} fusion(f32[1,64,64]{2,1,0:T(8,128)S(1)} %copy-done, f32[2,1,64,64]{3,2,1,0:T(8,128)S(1)} %get-tuple-element.4, f32[]{:T(128)} %bitcast.30, f32[]{:T(128)} %bitcast), kind=kLoop, calls=%fused_computation.4 | loop fusion | flops 20480 | bytes 65544 | tf_op jit(solution)/shard_map/sub | solution.py:408
Async XLA Ops:
  0.6 0.8 %copy-start = (f32[1,64,64]{2,1,0:T(8,128)S(1)}, f32[1,64,64]{2,1,0:T(8,128)}, u32[]{:S(2)}) copy-start(f32[1,64,64]{2,1,0:T(8,128)} %latent_hbm.1) | copy-start | bytes 49156
  1.4 0.7 %copy-start.1 = (s32[1,64]{1,0:T(1,128)S(1)}, s32[1,64]{1,0:T(1,128)}, u32[]{:S(2)}) copy-start(s32[1,64]{1,0:T(1,128)} %dest_ref.1) | copy-start | bytes 772

commit v3 on v1

--- a/solution.py
+++ b/solution.py
@@ -241,40 +241,48 @@
 
     left = lax.broadcasted_iota(jnp.int32, (cap // 2, 2 * channels), 1) < channels
 
-    for item in range(items):
-        pltpu.make_async_copy(heads_buf.at[item], heads_buf.at[item], head_recv.at[item]).wait()
-
-        block = min(keys_total, 256)
-
-        key_rows = heads_buf[item, :, 1].reshape(keys_total, HD)
-        value_rows = heads_buf[item, :, 2].reshape(keys_total, HD)
-        ranks = block // rows
+    together = 2 if items % 2 == 0 else 1
+    block = min(keys_total, 256)
+    ranks = block // rows
+    for first in range(0, items, together):
+        heads = range(first, first + together)
+        for item in heads:
+            pltpu.make_async_copy(
+                heads_buf.at[item], heads_buf.at[item], head_recv.at[item]
+            ).wait()
 
         def attend(index):
             at = pl.ds(pl.multiple_of(index * block, block), block)
-            query_rows = heads_buf[item, pl.ds(index * ranks, ranks), 0].reshape(block, HD)
-            scores = (
+            scores = [
                 lax.dot_general(
-                    query_rows,
-                    key_rows,
+                    heads_buf[item, pl.ds(index * ranks, ranks), 0].reshape(block, HD),
+                    heads_buf[item, :, 1].reshape(keys_total, HD),
                     (((1,), (1,)), ((), ())),
                     preferred_element_type=jnp.float32,
                 )
                 * scale
-            )
-            scores = jnp.where(live, scores, NEG_BIG)
-            weights = jnp.exp(scores - jnp.max(scores, axis=-1, keepdims=True))
-            inverse = 1.0 / jnp.sum(weights, axis=-1, keepdims=True)
-            probs = (weights * inverse).astype(jnp.bfloat16)
-            attended = jnp.dot(
-                probs, value_rows, preferred_element_type=jnp.float32
-            ).astype(jnp.bfloat16)
+                for item in heads
+            ]
+            scores = [jnp.where(live, s, NEG_BIG) for s in scores]
+            weights = [jnp.exp(s - jnp.max(s, axis=-1, keepdims=True)) for s in scores]
+            probs = [
+                (w * (1.0 / jnp.sum(w, axis=-1, keepdims=True))).astype(jnp.bfloat16)
+                for w in weights
+            ]
+            attended = [
+                jnp.dot(
+                    p,
+                    heads_buf[item, :, 2].reshape(keys_total, HD),
+                    preferred_element_type=jnp.float32,
+                ).astype(jnp.bfloat16)
+                for p, item in zip(probs, heads)
+            ]
             term = jnp.dot(
-                attended,
-                weight_rows[item * HD : (item + 1) * HD, :],
+                jnp.concatenate(attended, axis=1),
+                weight_rows[first * HD : (first + together) * HD, :],
                 preferred_element_type=jnp.float32,
             )
-            if item == 0:
+            if first == 0:
                 total[at, :] = term
             else:
                 total[at, :] += term

time: 25.2 us -> 25.2 us (level)
  no operation moved by 1% of the time
where the time goes in v3:
time: 25.2 us; the launch traced here: 24.9 us
  Pallas kernels  21 us (83%)
  between operations  2.05 us (8%)
  other arithmetic  1.23 us (5%)
  local copies, waits for them, and re-layouts  0.65 us (3%)
    pallas_call x1, Pallas kernels, local(): pl.pallas_call(functools.partial(kernel, n, items, videos), out_shape=(ja...  21 us
    unnamed x4, local copies, waits for them, and re-layouts  0.65 us
    sub x1, other arithmetic, local(): denoised = latents - sigma_now[:, None, None] * velocity  0.62 us
    add x1, other arithmetic, local(): merged_next = slots[2] + (sigma_next - sigma_now)[:, None, None] * merged  0.61 us

profile of v3, /device:TPU:0, one launch (start us, length us, event | category | flops | bytes accessed | tf_op | source)
XLA Modules:
  0.0 24.9 jit_solution(15759523840924160532)
XLA Ops:
  0.6 0.0 copy-start
  1.4 0.0 copy-start.1
  1.4 0.0 copy-done
  1.4 0.6 %copy-done.1 = s32[1,64]{1,0:T(1,128)S(1)} copy-done((s32[1,64]{1,0:T(1,128)S(1)}, s32[1,64]{1,0:T(1,128)}, u32[]{:S(2)}) %copy-start.1) | copy-done | bytes 280
  2.0 21.0 %shard_map.95 = (f32[2,1,64,64]{3,2,1,0:T(8,128)S(1)}, f32[3,1,16,64]{3,2,1,0:T(8,128)S(1)}) custom-call(bf16[32,4096]{1,0:T(8,128)(2,1)} %query_hbm.1, bf16[32,4096]{1,0:T(8,128)(2,1)} %key_hbm.1, bf16[32,4096]{1,0:T(8,128)(2,1)} %value_hbm.1, s32[1,64]{1,0:T(1,128)S(1)} %copy-done.1, f32[1,64,64]{2,1,0:T(8,128)S(1)} %copy-done, bf16[64,4096]{1,0:T(8,128)(2,1)} %bitcast.32), custom_call_target="tpu_custom_call" | custom-call | tf_op jit(solution)/shard_map/pallas_call | solution.py:360
  23.7 0.6 %fusion.7 = f32[1,16,64]{2,1,0:T(8,128)} fusion(f32[3,1,16,64]{3,2,1,0:T(8,128)S(1)} %get-tuple-element.5, f32[]{:T(128)} %bitcast.31, f32[]{:T(128)} %bitcast.6), kind=kLoop, calls=%fused_computation.9 | loop fusion | flops 5120 | bytes 16392 | tf_op jit(solution)/shard_map/add | solution.py:406
  24.3 0.6 %fusion.3 = f32[1,64,64]{2,1,0:T(8,128)} fusion(f32[1,64,64]{2,1,0:T(8,128)S(1)} %copy-done, f32[2,1,64,64]{3,2,1,0:T(8,128)S(1)} %get-tuple-element.4, f32[]{:T(128)} %bitcast.30, f32[]{:T(128)} %bitcast), kind=kLoop, calls=%fused_computation.4 | loop fusion | flops 20480 | bytes 65544 | tf_op jit(solution)/shard_map/sub | solution.py:404
Async XLA Ops:
  0.6 0.8 %copy-start = (f32[1,64,64]{2,1,0:T(8,128)S(1)}, f32[1,64,64]{2,1,0:T(8,128)}, u32[]{:S(2)}) copy-start(f32[1,64,64]{2,1,0:T(8,128)} %latent_hbm.1) | copy-start | bytes 49156
  1.4 0.7 %copy-start.1 = (s32[1,64]{1,0:T(1,128)S(1)}, s32[1,64]{1,0:T(1,128)}, u32[]{:S(2)}) copy-start(s32[1,64]{1,0:T(1,128)} %dest_ref.1) | copy-start | bytes 772
